TPU v7x, 256 devices: a whole 4x4x8 slice. The times are simulated.
256 devices in a mesh: seq: 64 (over x, z, core), head: 4 (over y).
Axes of the slice: x: 4, y: 4, z: 8, core: 2. Of those that a mesh axis runs over, the one named last changes fastest.
Arguments:
- queries: bfloat16 [65536, 2048], P('seq', 'head'), may hold values from -1.796875 to 1.796875
- keys: bfloat16 [65536, 2048], P('seq', 'head'), may hold values from -1.796875 to 1.796875
- values: bfloat16 [65536, 2048], P('seq', 'head'), may hold values from -16 to 16
- grad_out: bfloat16 [65536, 2048], P('seq', 'head'), may hold values from -1.1953125 to 1.1953125
Outputs:
- output: bfloat16 [65536, 2048], P('seq', 'head')
- grad_query: bfloat16 [65536, 2048], P('seq', 'head')
- grad_key: bfloat16 [65536, 2048], P('seq', 'head')
- grad_value: bfloat16 [65536, 2048], P('seq', 'head')
All inputs are finite; a program needn't handle non-finite values.
Results may differ from a plain program's by a relative error of at most 0.0065.
Values sent between devices are 32-bit elements; how exact they have to be, the bound alone decides.
A program may use at most 128 MiB of HBM per device.

v0:
```python
import jax
import jax.numpy as jnp
from jax import lax
from jax.sharding import PartitionSpec as P

HEADS = 16
HEAD_DIM = 128
EPSILON = 1e-06


def entering(shard, axis, combine, identity, reverse):
    size, here = (lax.axis_size(axis), lax.axis_index(axis))
    everything = lax.all_gather(shard, axis)
    start = jnp.broadcast_to(jnp.asarray(identity, shard.dtype), shard.shape)

    def step(k, before):
        at = size - 1 - k if reverse else k
        reached = at > here if reverse else at < here
        new = combine(before, everything[at])
        return jnp.where(reached, new, before)

    return lax.fori_loop(0, size, step, start)


def add_states(earlier, later):
    return earlier + later


def masked_scores(query_side, key_side):
    raw_scores = jnp.einsum(
        "thd,shd->hts", query_side, key_side, preferred_element_type=jnp.float32
    )
    count = query_side.shape[0]
    row_index = lax.broadcasted_iota(jnp.int32, (count, count), 0)
    col_index = lax.broadcasted_iota(jnp.int32, (count, count), 1)
    keep = (row_index >= col_index)[None]
    return jnp.where(keep, raw_scores, jnp.zeros_like(raw_scores)).astype(jnp.bfloat16)


def shards(queries, keys, values, grad_out):
    tok_rows = queries.shape[0]
    local_heads = queries.shape[1] // HEAD_DIM
    shaped = (tok_rows, local_heads, HEAD_DIM)
    full_width = HEADS * HEAD_DIM
    query_rows = queries.reshape(shaped)
    key_rows = keys.reshape(shaped)
    value_rows = values.reshape(shaped)
    local_state = jnp.einsum(
        "thd,the->hde", key_rows, value_rows, preferred_element_type=jnp.float32
    )
    zero_state = jnp.zeros_like(local_state)
    prefix = entering(local_state, "seq", add_states, zero_state, False)
    scores = masked_scores(query_rows, key_rows)
    prefix_round = prefix.astype(jnp.bfloat16)
    mixed = jnp.einsum("hts,she->the", scores, value_rows, preferred_element_type=jnp.float32)
    mixed = mixed + jnp.einsum(
        "thd,hde->the", query_rows, prefix_round, preferred_element_type=jnp.float32
    )
    mixed_rows = mixed.reshape(tok_rows, -1)
    grad_float = grad_out.astype(jnp.float32)
    squares = lax.psum(jnp.sum(mixed_rows * mixed_rows, axis=1), "head")
    inverse_rms = lax.rsqrt(squares / full_width + EPSILON)
    normed = mixed_rows * inverse_rms[:, None]
    crossed = lax.psum(jnp.sum(grad_float * normed, axis=1), "head")
    cross_mean = (crossed / full_width)[:, None]
    output = normed.astype(jnp.bfloat16)
    grad_mixed = (
        (inverse_rms[:, None] * (grad_float - normed * cross_mean))
        .astype(jnp.bfloat16)
        .reshape(shaped)
    )
    grad_state = jnp.einsum(
        "thd,the->hde", query_rows, grad_mixed, preferred_element_type=jnp.float32
    )
    suffix = entering(grad_state, "seq", add_states, zero_state, True)
    suffix_round = suffix.astype(jnp.bfloat16)
    grad_scores = masked_scores(grad_mixed, value_rows)
    grad_q = jnp.einsum("hts,shd->thd", grad_scores, key_rows, preferred_element_type=jnp.float32)
    grad_q = grad_q + jnp.einsum(
        "the,hde->thd", grad_mixed, prefix_round, preferred_element_type=jnp.float32
    )
    grad_k = jnp.einsum("hts,thd->shd", grad_scores, query_rows, preferred_element_type=jnp.float32)
    grad_k = grad_k + jnp.einsum(
        "she,hde->shd", value_rows, suffix_round, preferred_element_type=jnp.float32
    )
    grad_v = jnp.einsum("hts,the->she", scores, grad_mixed, preferred_element_type=jnp.float32)
    grad_v = grad_v + jnp.einsum(
        "shd,hde->she", key_rows, suffix_round, preferred_element_type=jnp.float32
    )
    flat_shape = (tok_rows, local_heads * HEAD_DIM)
    return (
        output,
        grad_q.astype(jnp.bfloat16).reshape(flat_shape),
        grad_k.astype(jnp.bfloat16).reshape(flat_shape),
        grad_v.astype(jnp.bfloat16).reshape(flat_shape),
    )


def solution(mesh):
    return jax.shard_map(
        shards,
        mesh=mesh,
        in_specs=(P("seq", "head"), P("seq", "head"), P("seq", "head"), P("seq", "head")),
        out_specs=(P("seq", "head"), P("seq", "head"), P("seq", "head"), P("seq", "head")),
        check_vma=False,
    )
```

profile of v0, /device:TPU:1, one launch (start us, length us, event | category | flops | bytes accessed | tf_op | source)
XLA Modules:
  0.0 399.9 jit_solution(9009849528236782950)
XLA Ops:
  7.2 2.4 copy.100
  9.6 2.4 fusion.10
  13.5 2.5 select_convert_fusion.1
  16.0 3.2 copy-done.1
  19.3 2.9 fusion.5
  22.2 94.0 %all-gather.5.cloned.1.call-done = f32[256,128,128]{2,1,0:T(8,128)} async-done(((f32[4,128,128]{2,1,0:T(8,128)}), f32[256,128,128]{2,1,0:T(8,128)}) %all-gather.5.cloned.1.call-update) | async-done | bytes 16777232 | tf_op jit(solution)/shard_map/all_gather | solution.py:13
  116.2 68.1 %while.30 = (s32[]{:T(128)}, f32[4,128,128]{2,1,0:T(8,128)S(1)}, s32[]{:T(128)}, f32[64,4,128,128]{3,2,1,0:T(8,128)}, s32[]{:T(128)}, /*index=5*/s32[]{:T(128)}) while((s32[]{:T(128)}, f32[4,128,128]{2,1,0:T(8,128)S(1)}, s32[]{:T(128)}, f32[64,4,128,128]{3,2,1,0:T(8,128)}, s32[]{:T(128)}, /*index=5*/s32[]{:T(128)}) %tuple.87), condition=%wide.region_1.2_spmd.clone, body=%wide.region_0.1_spmd.clone.sunk | while | flops 196612 | bytes 786533 | solution.py:22
  117.2 1.0 add_select_fusion.4
  119.3 1.0 add_select_fusion.4
  121.5 1.0 add_select_fusion.4
  123.6 1.0 add_select_fusion.4
  125.7 1.0 add_select_fusion.4
  127.9 1.0 add_select_fusion.4
  137.4 1.0 add_select_fusion.4
  139.6 1.0 add_select_fusion.4
  141.7 1.0 add_select_fusion.4
  143.8 1.0 add_select_fusion.4
  146.0 1.0 add_select_fusion.4
  148.1 1.0 add_select_fusion.4
  157.7 1.0 add_select_fusion.4
  159.8 1.0 add_select_fusion.4
  161.9 1.0 add_select_fusion.4
  164.0 1.0 add_select_fusion.4
  166.2 1.0 add_select_fusion.4
  168.3 1.0 add_select_fusion.4
  177.9 1.0 add_select_fusion.4
  180.0 1.0 add_select_fusion.4
  182.1 1.0 add_select_fusion.4
  184.3 1.8 multiply_reduce_fusion
  186.1 8.4 %psum.14 = f32[1024]{0:T(1024)S(1)} all-reduce(f32[1024]{0:T(1024)S(1)} %get-tuple-element.255), channel_id=1, replica_groups=mesh['seq'=64,'head'=4] {'head'}, use_global_device_ids=true, to_apply=%region_3.4 | all-reduce | flops 1024 | bytes 8192 | tf_op jit(solution)/shard_map/psum | solution.py:61
  194.5 1.9 copy.38
  196.5 1.7 fusion
  198.2 6.0 %psum.15 = f32[1024]{0:T(1024)S(1)} all-reduce(f32[1024]{0:T(1024)S(1)} %fusion), channel_id=1, replica_groups=mesh['seq'=64,'head'=4] {'head'}, use_global_device_ids=true, to_apply=%region_5.6 | all-reduce | flops 1024 | bytes 8192 | tf_op jit(solution)/shard_map/psum | solution.py:64
  204.2 3.0 fusion.2
  207.2 1.5 copy.56
  210.0 4.3 %select_convert_fusion = bf16[4,1024,1024]{2,1,0:T(8,128)(2,1)S(1)} fusion(bf16[1024,4,128]{0,2,1:T(8,128)(2,1)S(1)} %bitcast.105, pred[1024,1024]{1,0:T(8,128)(4,1)} %copy-done.10, bf16[1024,512]{1,0:T(8,128)(2,1)} %param.10), kind=kOutput, calls=%fused_computation.2 | convolution fusion | flops 1082130432 | bytes 11534336 | tf_op jit(solution)/shard_map/thd,shd->hts/dot_general | solution.py:30
  214.4 2.9 fusion.32
  217.6 1.4 fusion.4
  219.0 2.3 copy.51
  221.3 6.2 %fusion.33 = f32[4,128,1024]{2,1,0:T(8,128)} fusion(bf16[1024,4,128]{0,2,1:T(8,128)(2,1)S(1)} %bitcast.107, bf16[4,1024,1024]{2,1,0:T(8,128)(2,1)} %copy-done.1), kind=kOutput, calls=%fused_computation.49 | convolution fusion | flops 1073741824 | bytes 11534336 | tf_op jit(solution)/shard_map/hts,the->she/dot_general | solution.py:86
  227.5 82.1 %all-gather.7.cloned.1.call-done = f32[256,128,128]{2,1,0:T(8,128)} async-done(((f32[4,128,128]{2,1,0:T(8,128)}), f32[256,128,128]{2,1,0:T(8,128)}) %all-gather.7.cloned.1.call-update) | async-done | bytes 16777232 | tf_op jit(solution)/shard_map/all_gather | solution.py:13
  309.6 68.4 %while.31 = (s32[]{:T(128)}, f32[4,128,128]{2,1,0:T(8,128)S(1)}, s32[]{:T(128)}, f32[64,4,128,128]{3,2,1,0:T(8,128)}, s32[]{:T(128)}, /*index=5*/s32[]{:T(128)}, s32[]{:T(128)}, s32[]{:T(128)}) while((s32[]{:T(128)}, f32[4,128,128]{2,1,0:T(8,128)S(1)}, s32[]{:T(128)}, f32[64,4,128,128]{3,2,1,0:T(8,128)}, s32[]{:T(128)}, ...), condition=%wide.region_7.8_spmd.clone, body=%wide.region_6.7_spmd.clone.sunk | while | flops 196616 | bytes 786595 | solution.py:22
  310.7 1.0 add_select_fusion.5
  378.0 3.2 fusion.7
  381.2 1.5 add_convert_fusion
  382.7 2.4 copy.53
  385.1 5.7 %fusion.3 = bf16[1024,4,128]{0,2,1:T(8,128)(2,1)} fusion(f32[4,128,1024]{2,1,0:T(8,128)S(1)} %copy-done.4, bf16[4,1024,1024]{2,1,0:T(8,128)(2,1)} %copy-done.2, bf16[1024,512]{1,0:T(8,128)(2,1)S(1)} %copy-done), kind=kOutput, calls=%fused_computation.11 | convolution fusion | flops 1074790400 | bytes 12582912 | tf_op jit(solution)/shard_map/hts,thd->shd/dot_general | solution.py:82
  390.8 2.3 copy.52
  (138 shorter events, 113.3 us)
Async XLA Ops:
  7.2 6.3 %copy-start = (bf16[1024,512]{1,0:T(8,128)(2,1)S(1)}, bf16[1024,512]{1,0:T(8,128)(2,1)}, u32[]{:S(2)}) copy-start(bf16[1024,512]{1,0:T(8,128)(2,1)} %param.8) | copy-start | bytes 3145732
  7.2 2.5 copy-start.7
  7.2 109.0 %all-gather.5.cloned.1.call-start = ((), (), s32[]{:S(2)}) async-start(), calls=%async_computation | async-start | bytes 17039360 | tf_op jit(solution)/shard_map/all_gather | solution.py:13
  9.6 3.8 copy-start.5
  12.1 297.5 %all-gather.7.cloned.1.call-start = ((), (), s32[]{:S(2)}) async-start(), calls=%async_computation.1 | async-start | bytes 17039360 | tf_op jit(solution)/shard_map/all_gather | solution.py:13
  12.5 1.0 copy-start.10
  13.5 5.8 %copy-start.8 = (bf16[1024,512]{1,0:T(8,128)(2,1)S(1)}, bf16[1024,512]{1,0:T(8,128)(2,1)}, u32[]{:S(2)}) copy-start(bf16[1024,512]{1,0:T(8,128)(2,1)} %param.10) | copy-start | bytes 3145732
  16.0 3.2 copy-start.1
  210.0 4.4 %copy-start.9 = (bf16[1024,512]{0,1:T(8,128)(2,1)S(1)}, bf16[1024,512]{0,1:T(8,128)(2,1)}, u32[]{:S(2)}) copy-start(bf16[1024,512]{0,1:T(8,128)(2,1)} %copy.100) | copy-start | bytes 3145732
  214.4 3.2 copy-start.2
  378.0 3.2 copy-start.3
  378.0 3.2 copy-start.6
  382.7 2.4 copy-start.4
Sparse Core Ops, SparseCore 0:
  12.2 103.8 all-gather.4
  210.1 99.4 all-gather.6
where the time goes:
time: 404 us; the launch traced here: 400 us
  waiting for transfers between devices  176 us (44%)
  other arithmetic  138 us (34%)
  matrix products  35.3 us (9%)
  local copies, waits for them, and re-layouts  18.2 us (5%)
  blocking collectives  14.4 us (4%)
  between operations  14.2 us (4%)
    all_gather x2, waiting for transfers between devices, entering(): everything = lax.all_gather(shard, axis)  176 us
    select_n x128, other arithmetic, step(): return jnp.where(reached, new, before)  133 us
    unnamed x25, local copies, waits for them, and re-layouts  11.5 us
    psum x1, blocking collectives, shards(): squares = lax.psum(jnp.sum(mixed_rows * mixed_rows, axis=1), 'head')  8.42 us
  transfers between devices with their start and end apart: 2, of which 2 were waited for; matrix products, arithmetic and copies ran while one was open for 6% of the time, Pallas kernels for 0%

commit v1 on v0

--- a/solution.py
+++ b/solution.py
@@ -58,7 +58,7 @@
     )
     mixed_rows = mixed.reshape(tok_rows, -1)
     grad_float = grad_out.astype(jnp.float32)
-    squares = lax.psum(jnp.sum(mixed_rows * mixed_rows, axis=1), "head")
+    squares = jnp.sum(lax.all_gather(jnp.sum(mixed_rows * mixed_rows, axis=1), "head"), axis=0)
     inverse_rms = lax.rsqrt(squares / full_width + EPSILON)
     normed = mixed_rows * inverse_rms[:, None]
     crossed = lax.psum(jnp.sum(grad_float * normed, axis=1), "head")

time: 404 us -> 407 us (level)
    all_gather x0 -> x1, blocking collectives: none -> 9.38 us  [shards(): lax.all_gather(jnp.sum(mixed_rows * mixed_rows, axis=1), 'head')]
    psum x1 -> x0, blocking collectives: 8.42 us -> none  [shards(): squares = lax.psum(jnp.sum(mixed_rows * mixed_rows, axis=1), 'head')]
where the time goes in v1:
time: 407 us; the launch traced here: 403 us
  waiting for transfers between devices  176 us (43%)
  other arithmetic  138 us (34%)
  matrix products  35.3 us (9%)
  local copies, waits for them, and re-layouts  18.2 us (4%)
  blocking collectives  17.5 us (4%)
  between operations  14.2 us (3%)
    all_gather x2, waiting for transfers between devices, entering(): everything = lax.all_gather(shard, axis)  176 us
    select_n x128, other arithmetic, step(): return jnp.where(reached, new, before)  133 us
    unnamed x25, local copies, waits for them, and re-layouts  11.5 us
    all_gather x1, blocking collectives, shards(): lax.all_gather(jnp.sum(mixed_rows * mixed_rows, axis=1), 'head')  9.38 us
  transfers between devices with their start and end apart: 2, of which 2 were waited for; matrix products, arithmetic and copies ran while one was open for 6% of the time, Pallas kernels for 0%

profile of v1, /device:TPU:1, one launch (start us, length us, event | category | flops | bytes accessed | tf_op | source)
XLA Modules:
  0.0 403.0 jit_solution(1154528701728091022)
XLA Ops:
  7.2 2.4 copy.123
  9.6 2.4 fusion.10
  13.5 2.5 select_convert_fusion.1
  16.0 3.2 copy-done.1
  19.3 2.9 fusion.5
  22.2 94.0 %all-gather.6.cloned.1.call-done = f32[256,128,128]{2,1,0:T(8,128)} async-done(((f32[4,128,128]{2,1,0:T(8,128)}), f32[256,128,128]{2,1,0:T(8,128)}) %all-gather.6.cloned.1.call-update) | async-done | bytes 16777232 | tf_op jit(solution)/shard_map/all_gather | solution.py:13
  116.2 68.1 %while.30 = (s32[]{:T(128)}, f32[4,128,128]{2,1,0:T(8,128)S(1)}, s32[]{:T(128)}, f32[64,4,128,128]{3,2,1,0:T(8,128)}, s32[]{:T(128)}, /*index=5*/s32[]{:T(128)}) while((s32[]{:T(128)}, f32[4,128,128]{2,1,0:T(8,128)S(1)}, s32[]{:T(128)}, f32[64,4,128,128]{3,2,1,0:T(8,128)}, s32[]{:T(128)}, /*index=5*/s32[]{:T(128)}) %tuple.88), condition=%wide.region_1.2_spmd.clone, body=%wide.region_0.1_spmd.clone.sunk | while | flops 196612 | bytes 786533 | solution.py:22
  117.2 1.0 add_select_fusion.4
  119.3 1.0 add_select_fusion.4
  121.5 1.0 add_select_fusion.4
  123.6 1.0 add_select_fusion.4
  125.7 1.0 add_select_fusion.4
  127.9 1.0 add_select_fusion.4
  137.4 1.0 add_select_fusion.4
  139.6 1.0 add_select_fusion.4
  141.7 1.0 add_select_fusion.4
  143.8 1.0 add_select_fusion.4
  146.0 1.0 add_select_fusion.4
  148.1 1.0 add_select_fusion.4
  157.7 1.0 add_select_fusion.4
  159.8 1.0 add_select_fusion.4
  161.9 1.0 add_select_fusion.4
  164.0 1.0 add_select_fusion.4
  166.2 1.0 add_select_fusion.4
  168.3 1.0 add_select_fusion.4
  177.9 1.0 add_select_fusion.4
  180.0 1.0 add_select_fusion.4
  182.1 1.0 add_select_fusion.4
  184.3 1.8 multiply_reduce_fusion
  186.1 1.9 copy.61
  188.0 9.4 %all-gather.1 = f32[4096]{0:T(1024)S(1)} all-gather(f32[1024]{0:T(1024)S(1)} %get-tuple-element.259), channel_id=3, replica_groups=mesh['seq'=64,'head'=4] {'head'}, dimensions={0}, use_global_device_ids=true | all-gather | bytes 20480 | tf_op jit(solution)/shard_map/all_gather | solution.py:61
  197.4 1.7 fusion
  199.2 8.1 %psum.7 = f32[1024]{0:T(1024)S(1)} all-reduce(f32[1024]{0:T(1024)S(1)} %fusion), channel_id=1, replica_groups=mesh['seq'=64,'head'=4] {'head'}, use_global_device_ids=true, to_apply=%region_5.6 | all-reduce | flops 1024 | bytes 8192 | tf_op jit(solution)/shard_map/psum | solution.py:64
  207.3 3.0 fusion.2
  210.3 1.5 copy.79
  213.1 4.3 %select_convert_fusion = bf16[4,1024,1024]{2,1,0:T(8,128)(2,1)S(1)} fusion(bf16[1024,4,128]{0,2,1:T(8,128)(2,1)S(1)} %bitcast.105, pred[1024,1024]{1,0:T(8,128)(4,1)} %copy-done.10, bf16[1024,512]{1,0:T(8,128)(2,1)} %param.10), kind=kOutput, calls=%fused_computation.2 | convolution fusion | flops 1082130432 | bytes 11534336 | tf_op jit(solution)/shard_map/thd,shd->hts/dot_general | solution.py:30
  217.5 2.9 fusion.32
  220.7 1.4 fusion.4
  222.1 2.3 copy.74
  224.4 6.2 %fusion.33 = f32[4,128,1024]{2,1,0:T(8,128)} fusion(bf16[1024,4,128]{0,2,1:T(8,128)(2,1)S(1)} %bitcast.107, bf16[4,1024,1024]{2,1,0:T(8,128)(2,1)} %copy-done.1), kind=kOutput, calls=%fused_computation.49 | convolution fusion | flops 1073741824 | bytes 11534336 | tf_op jit(solution)/shard_map/hts,the->she/dot_general | solution.py:86
  230.6 82.1 %all-gather.8.cloned.1.call-done = f32[256,128,128]{2,1,0:T(8,128)} async-done(((f32[4,128,128]{2,1,0:T(8,128)}), f32[256,128,128]{2,1,0:T(8,128)}) %all-gather.8.cloned.1.call-update) | async-done | bytes 16777232 | tf_op jit(solution)/shard_map/all_gather | solution.py:13
  312.7 68.4 %while.31 = (s32[]{:T(128)}, f32[4,128,128]{2,1,0:T(8,128)S(1)}, s32[]{:T(128)}, f32[64,4,128,128]{3,2,1,0:T(8,128)}, s32[]{:T(128)}, /*index=5*/s32[]{:T(128)}, s32[]{:T(128)}, s32[]{:T(128)}) while((s32[]{:T(128)}, f32[4,128,128]{2,1,0:T(8,128)S(1)}, s32[]{:T(128)}, f32[64,4,128,128]{3,2,1,0:T(8,128)}, s32[]{:T(128)}, ...), condition=%wide.region_7.8_spmd.clone, body=%wide.region_6.7_spmd.clone.sunk | while | flops 196616 | bytes 786595 | solution.py:22
  313.8 1.0 add_select_fusion.5
  381.1 3.2 fusion.7
  384.3 1.5 add_convert_fusion
  385.7 2.4 copy.76
  388.2 5.7 %fusion.3 = bf16[1024,4,128]{0,2,1:T(8,128)(2,1)} fusion(f32[4,128,1024]{2,1,0:T(8,128)S(1)} %copy-done.4, bf16[4,1024,1024]{2,1,0:T(8,128)(2,1)} %copy-done.2, bf16[1024,512]{1,0:T(8,128)(2,1)S(1)} %copy-done), kind=kOutput, calls=%fused_computation.11 | convolution fusion | flops 1074790400 | bytes 12582912 | tf_op jit(solution)/shard_map/hts,thd->shd/dot_general | solution.py:82
  393.9 2.3 copy.75
  (140 shorter events, 113.3 us)
Async XLA Ops:
  7.2 6.3 %copy-start = (bf16[1024,512]{1,0:T(8,128)(2,1)S(1)}, bf16[1024,512]{1,0:T(8,128)(2,1)}, u32[]{:S(2)}) copy-start(bf16[1024,512]{1,0:T(8,128)(2,1)} %param.8) | copy-start | bytes 3145732
  7.2 2.5 copy-start.7
  7.2 109.0 %all-gather.6.cloned.1.call-start = ((), (), s32[]{:S(2)}) async-start(), calls=%async_computation | async-start | bytes 17039360 | tf_op jit(solution)/shard_map/all_gather | solution.py:13
  9.6 3.8 copy-start.5
  12.1 300.6 %all-gather.8.cloned.1.call-start = ((), (), s32[]{:S(2)}) async-start(), calls=%async_computation.1 | async-start | bytes 17039360 | tf_op jit(solution)/shard_map/all_gather | solution.py:13
  12.5 1.0 copy-start.10
  13.5 5.8 %copy-start.8 = (bf16[1024,512]{1,0:T(8,128)(2,1)S(1)}, bf16[1024,512]{1,0:T(8,128)(2,1)}, u32[]{:S(2)}) copy-start(bf16[1024,512]{1,0:T(8,128)(2,1)} %param.10) | copy-start | bytes 3145732
  16.0 3.2 copy-start.1
  213.1 4.4 %copy-start.9 = (bf16[1024,512]{0,1:T(8,128)(2,1)S(1)}, bf16[1024,512]{0,1:T(8,128)(2,1)}, u32[]{:S(2)}) copy-start(bf16[1024,512]{0,1:T(8,128)(2,1)} %copy.123) | copy-start | bytes 3145732
  217.5 3.2 copy-start.2
  381.1 3.2 copy-start.3
  381.1 3.2 copy-start.6
  385.7 2.4 copy-start.4
Sparse Core Ops, SparseCore 0:
  12.2 103.8 all-gather.5
  213.2 99.4 all-gather.7
